TPU v7x, 512 devices: a whole 4x4x16 slice. The times are simulated.
512 devices in a mesh: row: 32 (over y, x, core), col: 16 (over z).
Axes of the slice: x: 4, y: 4, z: 16, core: 2. Of those that a mesh axis runs over, the one named last changes fastest.
Arguments:
- col_samples: float32 [64, 2, 2048, 128], P('row', None, 'col'), may hold values from -6 to 6
- row_samples: float32 [64, 2, 128, 2048], P('row', None, None, 'col'), may hold values from -6 to 6
- pivot_rows: int32 [64, 128], P('row'), may hold values from 0 to 2047
- rank_blocks: int32 [64], P('row'), may hold values from 1 to 8
- upper_inverse: float32 [2, 2048, 2048], P(None, 'col', 'row'), as said below
- upanel_left: float32 [16, 2, 2048, 128], P('col'), may hold values from -0.125 to 0.125
Outputs:
- panel_right: float32 [64, 2, 128, 2048], P('row', None, None, 'col')
- cores: float32 [64, 16, 2, 128, 128], P('row', 'col')
Inputs may be any that keep to these rules, and one draw needn't show every extreme that they name: `rank_blocks`: the tile's rank is 16 times this. `upper_inverse`: zero below the diagonal in both parts.
All inputs are finite; a program needn't handle non-finite values.
Results may differ from a plain program's by a relative error of at most 0.00007.
Values sent between devices are 32-bit elements; how exact they have to be, the bound alone decides.
No kernel may reach another device: no remote copies, remote signals or barrier semaphores. Data moves between devices by JAX's collectives and lax.ppermute only.
A program may use at most 64 MiB of HBM per device.

v0:
```python
import jax
import jax.numpy as jnp
from jax import lax
from jax.sharding import PartitionSpec as P

RANK_STEP = 16


def complex_product(pattern, left_real, left_imag, right_real, right_imag):

    def single(left, right):
        return jnp.einsum(
            pattern,
            left,
            right,
            precision=lax.Precision.HIGHEST,
            preferred_element_type=jnp.float32,
        )

    real_part = single(left_real, right_real) - single(left_imag, right_imag)
    imag_part = single(left_real, right_imag) + single(left_imag, right_real)
    return (real_part, imag_part)


def scale_rows(values, weight_real, weight_imag):
    wr = weight_real[:, :, None]
    wi = weight_imag[:, :, None]
    real_part = values[:, 0] * wr - values[:, 1] * wi
    imag_part = values[:, 0] * wi + values[:, 1] * wr
    return jnp.stack((real_part, imag_part), axis=1)


def on_device(col_samples, row_samples, pivot_rows, rank_blocks, upper_inverse, upanel_left):
    width_local = col_samples.shape[2]
    ranks_max = row_samples.shape[2]
    offset = lax.axis_index("col") * width_local
    positions = offset + lax.broadcasted_iota(jnp.int32, (1, 1, width_local), 2)
    hits = (pivot_rows[:, :, None] == positions).astype(jnp.float32)
    flipped = jnp.swapaxes(col_samples, 2, 3)
    partial_entries = jnp.sum(flipped * hits[:, None], axis=3)
    entries = lax.psum(partial_entries, "col")
    levels = lax.broadcasted_iota(jnp.int32, (1, ranks_max), 1)
    keeping = (levels < RANK_STEP * rank_blocks[:, None]).astype(jnp.float32)
    magnitude = jnp.maximum(entries[:, 0] * entries[:, 0] + entries[:, 1] * entries[:, 1], 1.0)
    factor_real = keeping * entries[:, 0] / magnitude
    factor_imag = -keeping * entries[:, 1] / magnitude
    scaled = scale_rows(row_samples, factor_real, factor_imag)
    portion = lax.all_gather(upper_inverse, "row", axis=2, tiled=True)
    real_part, imag_part = complex_product(
        "trk,kn->trn", scaled[:, 0], scaled[:, 1], portion[0], portion[1]
    )
    partial_panel = jnp.stack((real_part, imag_part), axis=1)
    panel_local = lax.psum_scatter(partial_panel, "col", scatter_dimension=3, tiled=True)
    portion = lax.all_gather(panel_local, "col", axis=3, tiled=True)
    core_real, core_imag = complex_product(
        "trn,jns->tjrs", portion[:, 0], portion[:, 1], upanel_left[:, 0], upanel_left[:, 1]
    )
    cores = jnp.stack((core_real, core_imag), axis=2)
    return (panel_local, cores)


def solution(mesh):
    in_specs = (
        P("row", None, "col", None),
        P("row", None, None, "col"),
        P("row", None),
        P("row"),
        P(None, "col", "row"),
        P("col", None, None, None),
    )
    out_specs = (P("row", None, None, "col"), P("row", "col", None, None, None))
    return jax.shard_map(
        on_device, mesh=mesh, in_specs=in_specs, out_specs=out_specs, check_vma=False
    )
```

profile of v0, /device:TPU:2, one launch (start us, length us, event | category | flops | bytes accessed | tf_op | source)
XLA Modules:
  0.0 281.9 jit_solution(7301261295972462733)
XLA Ops:
  7.2 0.0 all-gather.3.cloned.1.call-start
  7.2 1.5 copy.12
  8.8 0.0 reduce-scatter.2.cloned.1.call-start
  8.8 0.8 compare_convert_fusion
  9.6 1.0 fusion.18
  10.6 36.5 %psum.7 = f32[2,2,128]{2,1,0:T(2,128)S(1)} all-reduce(f32[2,2,128]{2,1,0:T(2,128)S(1)} %fusion.18), channel_id=1, replica_groups=mesh['row'=32,'col'=16] {'col'}, use_global_device_ids=true, to_apply=%region_1.0 | all-reduce | flops 512 | bytes 4096 | tf_op jit(solution)/shard_map/psum | solution.py:41
  47.1 0.7 broadcast_multiply_fusion
  47.8 0.1 select_divide_fusion
  47.8 27.1 %all-gather.3.cloned.1.call-done = f32[2,128,2048]{1,0,2:T(2,128)} async-done(((f32[2,128,64]{1,0,2:T(2,128)}), f32[2,128,2048]{1,0,2:T(2,128)}) %all-gather.3.cloned.1.call-update) | async-done | bytes 2097168 | tf_op jit(solution)/shard_map/all_gather | solution.py:48
  74.9 4.0 %fusion.25 = (f32[1,128,2048]{1,0,2:T(1,128)S(1)}, f32[1,128,2048]{1,0,2:T(1,128)S(1)}) fusion(f32[2,128,2048]{1,0,2:T(2,128)} %all-gather.3.cloned.1.call-done), kind=kLoop, calls=%fused_computation.41 | loop fusion | bytes 4194304 | tf_op jit(solution)/shard_map/slice | solution.py:50
  78.9 1.8 fusion.21
  80.8 1.8 fusion.23
  82.6 1.9 fusion
  84.5 1.9 fusion.1
  86.4 2.2 pad_maximum_fusion
  88.7 0.2 all-gather.5.cloned.1.call-start
  88.9 79.6 %reduce-scatter.2.cloned.1.call-done = f32[2,2,128,128]{3,2,0,1:T(8,128)} async-done(((f32[2,2,128,2048]{3,2,0,1:T(8,128)}), f32[2,2,128,128]{3,2,0,1:T(8,128)}) %reduce-scatter.2.cloned.1.call-update) | async-done | bytes 262160 | tf_op jit(solution)/shard_map/reduce_scatter | solution.py:53
  168.5 1.7 copy.15
  170.2 93.8 %all-gather.5.cloned.1.call-done = f32[2,2,128,2048]{3,2,0,1:T(8,128)} async-done(((f32[2,2,128,128]{3,2,0,1:T(8,128)}), f32[2,2,128,2048]{3,2,0,1:T(8,128)}) %all-gather.5.cloned.1.call-update) | async-done | bytes 4194320 | tf_op jit(solution)/shard_map/all_gather | solution.py:54
  263.9 3.6 %fusion.2 = f32[2,128,128]{2,1,0:T(8,128)S(1)} fusion(f32[2,2,128,2048]{3,2,0,1:T(8,128)} %all-gather.5.cloned.1.call-done, f32[1,2,2048,128]{3,2,1,0:T(8,128)S(1)} %copy-done.1), kind=kOutput, calls=%fused_computation.7 | convolution fusion | flops 805306368 | bytes 3276800 | tf_op jit(solution)/shard_map/trn,jns->tjrs/dot_general | solution.py:12
  267.5 3.4 %fusion.3 = f32[2,128,128]{2,1,0:T(8,128)S(1)} fusion(f32[2,2,128,2048]{3,2,0,1:T(8,128)} %all-gather.5.cloned.1.call-done, f32[1,2,2048,128]{3,2,1,0:T(8,128)S(1)} %copy-done.1), kind=kOutput, calls=%fused_computation.8 | convolution fusion | flops 805306368 | bytes 3276800 | tf_op jit(solution)/shard_map/trn,jns->tjrs/dot_general | solution.py:12
  270.9 1.8 fusion.9
  272.8 1.8 fusion.7
  274.6 0.7 copy.16
  (12 shorter events, 0.1 us)
Async XLA Ops:
  7.2 67.7 %all-gather.3.cloned.1.call-start = ((), (), s32[]{:S(2)}) async-start(), calls=%async_computation.1 | async-start | bytes 2162688 | tf_op jit(solution)/shard_map/all_gather | solution.py:48
  8.8 159.7 %reduce-scatter.2.cloned.1.call-start = ((), (), s32[]{:S(2)}) async-start(), calls=%async_computation.2 | async-start | bytes 4456448 | tf_op jit(solution)/shard_map/reduce_scatter | solution.py:53
  47.8 31.1 %copy-start.2 = (f32[2,2,128,128]{3,2,1,0:T(8,128)S(1)}, f32[2,2,128,128]{3,2,1,0:T(8,128)}, u32[]{:S(2)}) copy-start(f32[2,2,128,128]{3,2,1,0:T(8,128)} %param.7) | copy-start | bytes 786436
  88.6 175.3 %copy-start.1 = (f32[1,2,2048,128]{3,2,1,0:T(8,128)S(1)}, f32[1,2,2048,128]{3,2,1,0:T(8,128)}, u32[]{:S(2)}) copy-start(f32[1,2,2048,128]{3,2,1,0:T(8,128)} %param.11) | copy-start | bytes 6291460
  88.7 175.3 %all-gather.5.cloned.1.call-start = ((), (), s32[]{:S(2)}) async-start(), calls=%async_computation.3 | async-start | bytes 4456448 | tf_op jit(solution)/shard_map/all_gather | solution.py:54
  263.9 7.0 %copy-start = (f32[2,2,128,2048]{3,2,0,1:T(8,128)S(1)}, f32[2,2,128,2048]{3,2,0,1:T(8,128)}, u32[]{:S(2)}) copy-start(f32[2,2,128,2048]{3,2,0,1:T(8,128)} %all-gather.5.cloned.1.call-done) | copy-start | bytes 12582916
Sparse Core Ops, SparseCore 0:
  11.7 63.1 all-gather.2
  88.8 79.6 reduce-scatter.1
  170.5 93.4 all-gather.4
where the time goes:
time: 282 us
  waiting for transfers between devices  200 us (71%)
  blocking collectives  36.5 us (13%)
  matrix products  18.1 us (6%)
  between operations  13.9 us (5%)
  local copies, waits for them, and re-layouts  7.92 us (3%)
  other arithmetic  4.73 us (2%)
    all_gather x1, waiting for transfers between devices, on_device(): portion = lax.all_gather(panel_local, 'col', axis=3, tiled=True)  93.8 us
    reduce_scatter x1, waiting for transfers between devices, on_device(): lax.psum_scatter(partial_panel, 'col', scatter_dimension=3, tiled=True)  79.6 us
    psum x1, blocking collectives, on_device(): entries = lax.psum(partial_entries, 'col')  36.5 us
    all_gather x1, waiting for transfers between devices, on_device(): portion = lax.all_gather(upper_inverse, 'row', axis=2, tiled=True)  27.1 us
    dot_general x8, matrix products, single(): jnp.einsum(pattern, left, right, precision=lax.Precision.HIGHEST, preferr...  18.1 us
  transfers between devices with their start and end apart: 3, of which 3 were waited for; matrix products, arithmetic and copies ran while one was open for 1% of the time, Pallas kernels for 0%

commit v1 on v0

--- a/solution.py
+++ b/solution.py
@@ -45,7 +45,15 @@
     factor_real = keeping * entries[:, 0] / magnitude
     factor_imag = -keeping * entries[:, 1] / magnitude
     scaled = scale_rows(row_samples, factor_real, factor_imag)
-    portion = lax.all_gather(upper_inverse, "row", axis=2, tiled=True)
+    portion = jnp.concatenate(
+        jax.lax.all_to_all(
+            jnp.stack([upper_inverse for _ in range(jax.lax.axis_size("row"))]),
+            axis_name="row",
+            split_axis=0,
+            concat_axis=0,
+        ),
+        axis=2,
+    )
     real_part, imag_part = complex_product(
         "trk,kn->trn", scaled[:, 0], scaled[:, 1], portion[0], portion[1]
     )

time: 282 us -> 255 us (0.904)
  waiting for transfers between devices: 200 us -> 169 us
  starting transfers between devices: 0.3 us -> 9.97 us
    all_gather x1 -> x0, waiting for transfers between devices: 27.1 us -> none  [on_device(): portion = lax.all_gather(upper_inverse, 'row', axis=2, tiled=True)]
    all_to_all x0 -> x1, starting transfers between devices: none -> 9.71 us  [on_device(): jax.lax.all_to_all(jnp.stack([upper_inverse for _ in range(jax.lax.axis_s...]
    reduce_scatter x1, waiting for transfers between devices: 79.6 us -> 75.7 us  [on_device(): lax.psum_scatter(partial_panel, 'col', scatter_dimension=3, tiled=True)]
    slice x1, local copies, waits for them, and re-layouts: 4 us -> 0.24 us  [on_device(): portion[0]]
  transfers between devices with their start and end apart: 3 -> 3, of which waited for: 3 -> 2; matrix products, arithmetic and copies ran while one was open for 1% -> 1% of each run, Pallas kernels for 0% -> 0%
where the time goes in v1:
time: 255 us
  waiting for transfers between devices  169 us (66%)
  blocking collectives  34.5 us (14%)
  matrix products  18.1 us (7%)
  between operations  14.2 us (6%)
  starting transfers between devices  9.97 us (4%)
  local copies, waits for them, and re-layouts  6.03 us (2%)
    all_gather x1, waiting for transfers between devices, on_device(): portion = lax.all_gather(panel_local, 'col', axis=3, tiled=True)  93.8 us
    reduce_scatter x1, waiting for transfers between devices, on_device(): lax.psum_scatter(partial_panel, 'col', scatter_dimension=3, tiled=True)  75.7 us
    psum x1, blocking collectives, on_device(): entries = lax.psum(partial_entries, 'col')  34.5 us
    dot_general x8, matrix products, single(): jnp.einsum(pattern, left, right, precision=lax.Precision.HIGHEST, preferr...  18.1 us
    all_to_all x1, starting transfers between devices, on_device(): jax.lax.all_to_all(jnp.stack([upper_inverse for _ in range(jax.lax.axis_s...  9.71 us
  transfers between devices with their start and end apart: 3, of which 2 were waited for; matrix products, arithmetic and copies ran while one was open for 1% of the time, Pallas kernels for 0%

profile of v1, /device:TPU:2, one launch (start us, length us, event | category | flops | bytes accessed | tf_op | source)
XLA Modules:
  0.0 254.7 jit_solution(5950460007113735335)
XLA Ops:
  7.2 2.4 stack.14
  9.6 9.7 %all-to-all-start = ((f32[32,2,128,64]{2,3,1,0:T(8,128)}), f32[32,2,128,64]{2,3,1,0:T(8,128)S(1)}, u32[]{:S(2)}, u32[]{:S(2)}) async-start(f32[32,2,128,64]{2,3,1,0:T(8,128)} %stack.14), calls=%async_computation | async-start | bytes 4194304 | tf_op jit(solution)/shard_map/all_to_all | solution.py:49
  19.3 0.0 reduce-scatter.2.cloned.1.call-start
  19.4 0.1 compare_convert_fusion
  19.5 34.5 %psum.7 = f32[2,2,128]{2,1,0:T(2,128)S(1)} all-reduce(f32[2,2,128]{2,1,0:T(2,128)S(1)} %fusion.18), channel_id=1, replica_groups=mesh['row'=32,'col'=16] {'col'}, use_global_device_ids=true, to_apply=%region_1.0 | all-reduce | flops 512 | bytes 4096 | tf_op jit(solution)/shard_map/psum | solution.py:41
  54.1 0.1 select_divide_fusion
  54.2 0.2 copy.35
  54.4 0.2 fusion.25
  54.7 0.7 copy-done.2
  55.4 1.8 fusion.21
  57.2 1.8 fusion.23
  59.1 1.9 fusion
  61.0 1.9 fusion.1
  62.8 2.2 pad_maximum_fusion
  65.1 0.0 reduce-scatter.2.cloned.1.call-update
  65.1 0.2 all-gather.2.cloned.1.call-start
  65.3 75.7 %reduce-scatter.2.cloned.1.call-done = f32[2,2,128,128]{3,2,0,1:T(8,128)} async-done(((f32[2,2,128,2048]{3,2,0,1:T(8,128)}), f32[2,2,128,128]{3,2,0,1:T(8,128)}) %reduce-scatter.2.cloned.1.call-update) | async-done | bytes 262160 | tf_op jit(solution)/shard_map/reduce_scatter | solution.py:61
  141.0 1.7 copy.23
  142.7 93.8 %all-gather.2.cloned.1.call-done = f32[2,2,128,2048]{3,2,0,1:T(8,128)} async-done(((f32[2,2,128,128]{3,2,0,1:T(8,128)}), f32[2,2,128,2048]{3,2,0,1:T(8,128)}) %all-gather.2.cloned.1.call-update) | async-done | bytes 4194320 | tf_op jit(solution)/shard_map/all_gather | solution.py:62
  236.4 3.5 %fusion.2 = f32[2,128,128]{2,1,0:T(8,128)S(1)} fusion(f32[2,2,128,2048]{3,2,0,1:T(8,128)} %all-gather.2.cloned.1.call-done, f32[1,2,2048,128]{3,2,1,0:T(8,128)S(1)} %copy-done.1), kind=kOutput, calls=%fused_computation.8 | convolution fusion | flops 805306368 | bytes 3276800 | tf_op jit(solution)/shard_map/trn,jns->tjrs/dot_general | solution.py:12
  240.0 3.4 %fusion.3 = f32[2,128,128]{2,1,0:T(8,128)S(1)} fusion(f32[2,2,128,2048]{3,2,0,1:T(8,128)} %all-gather.2.cloned.1.call-done, f32[1,2,2048,128]{3,2,1,0:T(8,128)S(1)} %copy-done.1), kind=kOutput, calls=%fused_computation.9 | convolution fusion | flops 805306368 | bytes 3276800 | tf_op jit(solution)/shard_map/trn,jns->tjrs/dot_general | solution.py:12
  243.4 1.8 fusion.9
  245.3 1.8 fusion.7
  247.1 0.7 copy.24
  (18 shorter events, 0.1 us)
Async XLA Ops:
  9.6 9.8 %copy-start.4 = (s32[2,128]{1,0:T(2,128)S(1)}, s32[2,128]{1,0:T(2,128)}, u32[]{:S(2)}) copy-start(s32[2,128]{1,0:T(2,128)} %param.8) | copy-start | bytes 3076
  9.6 9.9 %copy-start.3 = (f32[2,2,128,128]{3,2,1,0:T(8,128)S(1)}, f32[2,2,128,128]{3,2,1,0:T(8,128)}, u32[]{:S(2)}) copy-start(f32[2,2,128,128]{3,2,1,0:T(8,128)} %param.6) | copy-start | bytes 786436
  9.6 44.5 %copy-start.5 = (s32[2]{0:T(128)S(1)}, s32[2]{0:T(128)}, u32[]{:S(2)}) copy-start(s32[2]{0:T(128)} %param.9) | copy-start | bytes 28
  9.6 44.6 %all-to-all-start = ((f32[32,2,128,64]{2,3,1,0:T(8,128)}), f32[32,2,128,64]{2,3,1,0:T(8,128)S(1)}, u32[]{:S(2)}, u32[]{:S(2)}) async-start(f32[32,2,128,64]{2,3,1,0:T(8,128)} %stack.14), calls=%async_computation | async-start | bytes 4194304 | tf_op jit(solution)/shard_map/all_to_all | solution.py:49
  19.3 121.6 %reduce-scatter.2.cloned.1.call-start = ((), (), s32[]{:S(2)}) async-start(), calls=%async_computation.2 | async-start | bytes 4456448 | tf_op jit(solution)/shard_map/reduce_scatter | solution.py:61
  54.4 1.0 copy-start.2
  65.1 171.4 %copy-start.1 = (f32[1,2,2048,128]{3,2,1,0:T(8,128)S(1)}, f32[1,2,2048,128]{3,2,1,0:T(8,128)}, u32[]{:S(2)}) copy-start(f32[1,2,2048,128]{3,2,1,0:T(8,128)} %param.11) | copy-start | bytes 6291460
  65.1 171.4 %all-gather.2.cloned.1.call-start = ((), (), s32[]{:S(2)}) async-start(), calls=%async_computation.3 | async-start | bytes 4456448 | tf_op jit(solution)/shard_map/all_gather | solution.py:62
  236.4 7.0 %copy-start = (f32[2,2,128,2048]{3,2,0,1:T(8,128)S(1)}, f32[2,2,128,2048]{3,2,0,1:T(8,128)}, u32[]{:S(2)}) copy-start(f32[2,2,128,2048]{3,2,0,1:T(8,128)} %all-gather.2.cloned.1.call-done) | copy-start | bytes 12582916
Sparse Core Ops, SparseCore 0:
  65.2 75.7 reduce-scatter.1
  143.0 93.4 all-gather.1
